TPU v7x, 512 devices: a whole 4x4x16 slice. The times are simulated.
512 devices in a mesh: dom: 128 (over z, x, core), narrow: 4 (over y).
Axes of the slice: x: 4, y: 4, z: 16, core: 2. Of those that a mesh axis runs over, the one named last changes fastest.
Arguments:
- state: float32 [13, 84, 131072], P(None, None, ('dom', 'narrow')), may hold values from -6 to 6
- predictor: float32 [13, 84, 131072], P(None, None, ('dom', 'narrow')), may hold values from -6 to 6
- degree: int32 [131072], P(('dom', 'narrow')), may hold values from 2 to 6
- material: int32 [131072], P(('dom', 'narrow')), may hold values from 0 to 31
- face_link: int32 [4, 131072], P(None, ('dom', 'narrow')), may hold values from 0 to 1407, as said below
- publish: int32 [4096], P(('dom', 'narrow')), may hold values from 0 to 255, as said below
- new_owner: int32 [131072], P(('dom', 'narrow')), may hold values from 0 to 127, as said below
- new_index: int32 [131072], P(('dom', 'narrow')), may hold values from 0 to 255, as said below
- derivative: float32 [3, 84, 84], replicated, may hold values from -0.625 to 0.625
- trace_ops: float32 [4, 28, 84], replicated, may hold values from -0.625 to 0.625
- lift_ops: float32 [4, 84, 28], replicated, may hold values from -0.5 to 0.5
- jacobians: float32 [32, 3, 13, 13], P('narrow'), may hold values from -1.75 to 1.75
- speeds: float32 [32], P('narrow'), may hold values from 0.5 to 3
- normals: float32 [3, 4, 131072], P(None, None, ('dom', 'narrow')), may hold values from -6 to 6
Outputs:
- corrected: float32 [13, 84, 131072], P(None, None, ('dom', 'narrow'))
- new_predictor: float32 [13, 84, 131072], P(None, None, ('dom', 'narrow'))
Inputs may be any that keep to these rules, and one draw needn't show every extreme that they name: `face_link`: values below 1024 name face v // 256 of element v % 256 of the same block; each of the 384 entries of a block's remote table is named by exactly one face of that block. `publish`: the 8 entries of one block are distinct element numbers of that block. Elements keep their narrow index. At most 4 elements of one device have the same new_owner, and in every draw some device sends exactly 4 to one dom index; every device receives exactly 256 elements. The elements that arrive at one device have distinct new_index.
All inputs are finite; a program needn't handle non-finite values.
Results may differ from a plain program's by a relative error of at most 0.0003.
Values sent between devices are 32-bit elements; how exact they have to be, the bound alone decides.
No kernel may reach another device: no remote copies, remote signals or barrier semaphores. Data moves between devices by JAX's collectives and lax.ppermute only.
A program may use at most 128 MiB of HBM per device.

v0:
```python
import functools
import jax
import jax.numpy as jnp
from jax import lax
from jax.experimental import pallas as pl
from jax.experimental.pallas import tpu as pltpu
from jax.sharding import PartitionSpec as P

time_step = 1.5
F = 13
M = 84
MS = 88
MP = 96
E = 256
QP = 32
AR = 176
SLOTS = 512
PAY = 1152
INFO = F * MS
PICK = F * 128
JROWS = 640
f32, bf16 = jnp.float32, jnp.bfloat16


def split(x):
    hi = x.astype(bf16)
    return hi, (x - hi.astype(f32)).astype(bf16)


def dot(a, b, contract=((1,), (0,))):
    return lax.dot_general(a, b, (contract, ((), ())), preferred_element_type=f32)


NT = ((1,), (1,))


def mode_rows(count):
    m = lax.broadcasted_iota(jnp.int32, (count, E), 0)
    deg = jnp.zeros((count, E), jnp.int32)
    for p in range(1, 7):
        deg = deg + (m >= p * (p + 1) * (p + 2) // 6).astype(jnp.int32)
    return jnp.where(m < M, deg, 99)


def keep_rows(degree_row, count):
    return (mode_rows(count) <= degree_row).astype(f32)


def pad_rows(x, rows):
    return jnp.concatenate([x, jnp.zeros((rows - x.shape[0], x.shape[1]), x.dtype)], axis=0)


def load_derivative(der_ref, scr):
    scr[...] = jnp.zeros(scr.shape, f32)
    for d in range(3):
        scr[d * MS : d * MS + M, 0:M] = der_ref[d]
    hi, lo = split(scr[:, 0:M])
    hi, lo = hi.astype(f32), lo.astype(f32)
    return jnp.concatenate([hi, hi, lo], axis=1).astype(bf16)


def slopes_into(x_ref, matrices, s_ref):
    for f in range(F):
        hi, lo = split(x_ref[f, 0:M, :])
        hi, lo = hi.astype(f32), lo.astype(f32)
        s_ref[f] = dot(matrices, jnp.concatenate([hi, lo, hi], axis=0).astype(bf16))


def apply_jacobian(s_ref, a_ref, half, blocks, finish):
    lanes = pl.ds(half * 128, 128)

    def body(i, carry):
        r = pl.multiple_of(i * 16, 16)
        acc = [[None] * F for _ in range(2)]
        for d in range(3):
            for f in range(F):
                x = [s_ref[f, pl.ds(d * MS + r + 8 * t, 8), lanes] for t in range(2)]
                for g in range(F):
                    w = jnp.broadcast_to(a_ref[pl.ds(d * AR + g * F + f, 1), lanes], (8, 128))
                    for t in range(2):
                        acc[t][g] = w * x[t] if acc[t][g] is None else acc[t][g] + w * x[t]
        for t in range(2):
            finish(pl.multiple_of(r + 8 * t, 8), lanes, acc[t])
        return carry

    lax.fori_loop(0, blocks, body, 0)


def material_matrix(jac_ref, onehot):
    table = jac_ref[...]
    hi = table.astype(bf16)
    rest = table - hi.astype(f32)
    mid, lo = split(rest)
    tn = ((0,), (0,))
    return dot(hi, onehot, tn) + dot(mid, onehot, tn) + dot(lo, onehot, tn)


def material_onehot(material_row, me):
    k = lax.broadcasted_iota(jnp.int32, (32, E), 0)
    ident = lax.rem(me - k // 8 + 4, 4) * 8 + k % 8
    return (ident == material_row).astype(f32).astype(bf16)


def pick_kernel(pred_ref, degree_ref, publish_ref, jac_ref, speed_ref, out_ref):
    keep = keep_rows(degree_ref[...], M)
    e = lax.broadcasted_iota(jnp.int32, (16, E), 1)
    onehot = (e == publish_ref[...]).astype(f32).astype(bf16)
    out_ref[...] = jnp.zeros(out_ref.shape, f32)
    for f in range(F):
        hi, lo = split(pred_ref[f] * keep)
        picked = dot(onehot, hi, NT) + dot(onehot, lo, NT)
        out_ref[:, f * 128 : f * 128 + M] = picked[0:8]
    for d in range(3):
        for g in range(F):
            at = PICK + d * AR + g * F
            out_ref[:, at : at + F] = jac_ref[d, g]
    out_ref[:, PICK + 3 * AR : PICK + 3 * AR + 1] = speed_ref[...]


def trace_matrix(trace_ref, scr):
    scr[...] = jnp.zeros(scr.shape, f32)
    for a in range(4):
        scr[a * QP : a * QP + 28, 0:M] = trace_ref[a]
    return split(scr[...])


def link_place(link, me):
    w = link - 4 * E
    block, a, j = w // 32, (w // 8) % 4, w % 8
    step = lax.rem(me - block % 4 + 4, 4)
    far = 4 * E + a * 128 + (block // 4) * 32 + step * 8 + j
    return jnp.where(link < 4 * E, link, far)


def trace_kernel(pred_ref, degree_ref, trace_ref, link_ref, own_ref, near_ref, tscr, both):
    keep = keep_rows(degree_ref[...], MP)
    thi, tlo = trace_matrix(trace_ref, tscr)
    thi, tlo = thi[:, 0:MP], tlo[:, 0:MP]
    thh = jnp.concatenate([thi, thi], axis=1)
    for f in range(F):
        x = pad_rows(pred_ref[f], MP) * keep
        hi, lo = split(x)
        t = dot(thh, jnp.concatenate([hi, lo], axis=0)) + dot(tlo, hi)
        for a in range(4):
            own_ref[a, f * QP : (f + 1) * QP, :] = t[a * QP : (a + 1) * QP]
    for a in range(4):
        hi, lo = split(own_ref[a])
        both[0 : F * QP, a * E : (a + 1) * E] = hi
        both[F * QP :, a * E : (a + 1) * E] = lo
    k = lax.broadcasted_iota(jnp.int32, (4 * E, E), 0)
    for a in range(4):
        onehot = (k == link_ref[a : a + 1, :]).astype(f32).astype(bf16)
        r = dot(both[...], onehot)
        near_ref[a] = r[0 : F * QP] + r[F * QP :]


def local_kernel(me_ref, state_ref, pred_ref, degree_ref, material_ref, jac_ref, der_ref, base_ref, a_ref, x, s, dscr):
    keep = keep_rows(degree_ref[...], MP)
    for f in range(F):
        x[f] = pad_rows(pred_ref[f], MP) * keep
    a_ref[...] = material_matrix(jac_ref, material_onehot(material_ref[...], me_ref[0]))
    slopes_into(x, load_derivative(der_ref, dscr), s)
    for f in range(F):
        base_ref[f] = pad_rows(state_ref[f], MP)

    def finish(r, lanes, acc):
        for g in range(F):
            base_ref[g, pl.ds(r, 8), lanes] = base_ref[g, pl.ds(r, 8), lanes] - acc[g]

    for half in range(2):
        apply_jacobian(s, a_ref, half, MP // 16, finish)


def flux_kernel(
    me_ref, own_ref, near_ref, base_ref, a_ref, pick_ref, link_ref, normals_ref, trace_ref, lift_ref, degree_ref, material_ref,
    owner_row_ref, owner_col_ref, index_ref, out_ref, tscr, far, outside, lscr, dirs, flux, u,
):
    me = me_ref[0]
    thi, tlo = trace_matrix(trace_ref, tscr)
    for f in range(F):
        phi, plo = split(pick_ref[:, f * 128 : (f + 1) * 128])
        t = dot(thi, phi, NT) + dot(thi, plo, NT) + dot(tlo, phi, NT)
        for a in range(4):
            far[f * QP : (f + 1) * QP, a * 128 : (a + 1) * 128] = t[a * QP : (a + 1) * QP]
    fhi, flo = split(far[...])
    both = jnp.concatenate([fhi, flo], axis=0)
    k = lax.broadcasted_iota(jnp.int32, (4 * 128, E), 0) + 4 * E
    for a in range(4):
        onehot = (k == link_place(link_ref[a : a + 1, :], me)).astype(f32).astype(bf16)
        r = dot(both, onehot)
        outside[a] = near_ref[a] + r[0 : F * QP] + r[F * QP :]
    speed = a_ref[3 * AR : 3 * AR + 1, :] * 0.5
    for a in range(4):
        total = normals_ref[0, a : a + 1, :] * a_ref[0:AR]
        for d in range(1, 3):
            total = total + normals_ref[d, a : a + 1, :] * a_ref[d * AR : (d + 1) * AR]
        dirs[a] = 0.5 * total

    def face(i, carry):
        a, lanes = i // 2, pl.ds(pl.multiple_of((i % 2) * 128, 128), 128)
        sp = a_ref[3 * AR : 3 * AR + 1, lanes] * 0.5
        for f0, f1 in ((0, 5), (5, 9), (9, 13)):
            acc = {}
            for f in range(f0, f1):
                for t in range(4):
                    rows = pl.ds(f * QP + t * 8, 8)
                    acc[f, t] = sp * (own_ref[a, rows, lanes] - outside[a, rows, lanes])
            for g in range(F):
                both_sides = [own_ref[a, pl.ds(g * QP + t * 8, 8), lanes] + outside[a, pl.ds(g * QP + t * 8, 8), lanes] for t in range(4)]
                for f in range(f0, f1):
                    w = jnp.broadcast_to(dirs[a, pl.ds(f * F + g, 1), lanes], (8, 128))
                    for t in range(4):
                        acc[f, t] = acc[f, t] + w * both_sides[t]
            for f in range(f0, f1):
                for t in range(4):
                    flux[f, pl.ds(a * QP + t * 8, 8), lanes] = acc[f, t]
        return carry

    lax.fori_loop(0, 8, face, 0)
    lscr[...] = jnp.zeros(lscr.shape, f32)
    for a in range(4):
        lscr[0:M, a * QP : a * QP + 28] = lift_ref[a]
    lhi, llo = split(lscr[...])
    lhh = jnp.concatenate([lhi, lhi], axis=1)
    keep = keep_rows(degree_ref[...], MS)
    for f in range(F):
        hi, lo = split(flux[f])
        lifted = dot(lhh, jnp.concatenate([hi, lo], axis=0)) + dot(llo, hi)
        u[f * MS : (f + 1) * MS, :] = (base_ref[f, 0:MS, :] - lifted[0:MS]) * keep
    u[INFO : INFO + 8, :] = jnp.concatenate(
        [degree_ref[...], material_ref[...], index_ref[...] + 1, jnp.zeros((5, E), jnp.int32)], axis=0
    ).astype(f32)
    owner = owner_row_ref[...]
    before = lax.broadcasted_iota(jnp.int32, (E, E), 0) < lax.broadcasted_iota(jnp.int32, (E, E), 1)
    rank = jnp.sum(jnp.where((owner_col_ref[...] == owner) & before, 1.0, 0.0), axis=0, keepdims=True)
    slot = owner * 4 + rank.astype(jnp.int32)
    pick = (lax.broadcasted_iota(jnp.int32, (SLOTS, E), 0) == slot).astype(f32).astype(bf16)
    for c in range(3):
        hi, lo = split(u[c * 384 : (c + 1) * 384, :])
        out_ref[:, :, c * 384 : (c + 1) * 384] = (dot(pick, hi, NT) + dot(pick, lo, NT)).reshape(SLOTS // 4, 4, 384)


def predict_kernel(me_ref, arrived_ref, jac_ref, der_ref, corrected_ref, ahead_ref, c, r, x, s, a, dscr, keep, ahead):
    arrived = arrived_ref[...].reshape(SLOTS, PAY)
    info = jnp.transpose(arrived[:, PAY - 128 :])
    lead = info[INFO - (PAY - 128) : INFO - (PAY - 128) + 1]
    slot_row = lax.broadcasted_iota(jnp.int32, (SLOTS, SLOTS), 1)
    slot_col = lax.broadcasted_iota(jnp.int32, (SLOTS, SLOTS), 0)
    degree_col = arrived[:, INFO : INFO + 1]
    ahead_of = (degree_col > lead) | ((degree_col == lead) & (slot_col < slot_row))
    rank = jnp.sum(jnp.where(ahead_of, 1.0, 0.0), axis=0, keepdims=True)
    rank = jnp.where(lead > 0, rank, -1.0).astype(jnp.int32)
    pick = (lax.broadcasted_iota(jnp.int32, (E, SLOTS), 0) == rank).astype(f32).astype(bf16)
    for i in range(3):
        hi, lo = split(arrived[:, i * 384 : (i + 1) * 384])
        r[:, i * 384 : (i + 1) * 384] = dot(pick, hi) + dot(pick, lo)
        c[i * 384 : (i + 1) * 384, :] = jnp.transpose(r[:, i * 384 : (i + 1) * 384])
    place = r[:, INFO + 2 : INFO + 3].astype(jnp.int32)
    spread = (lax.broadcasted_iota(jnp.int32, (E, E), 1) + 1 == place).astype(f32).astype(bf16)
    degree = c[INFO : INFO + 1, :].astype(jnp.int32)
    material = c[INFO + 1 : INFO + 2, :].astype(jnp.int32)
    a[...] = material_matrix(jac_ref, material_onehot(material, me_ref[0]))
    keep[...] = keep_rows(degree, MP)
    matrices = load_derivative(der_ref, dscr)
    for f in range(F):
        rows = c[f * MS : (f + 1) * MS, :]
        hi, lo = split(rows)
        corrected_ref[f] = (dot(hi, spread) + dot(lo, spread))[0:M]
        x[f] = pad_rows(rows, MP)
        ahead[f] = time_step * pad_rows(rows, MP)
    top = [jnp.max(degree[:, 128 * half : 128 * (half + 1)]) for half in range(2)]
    blocks = [jnp.where(t <= 2, 1, jnp.where(t == 3, 2, jnp.where(t == 4, 3, jnp.where(t == 5, 4, 6)))) for t in top]

    def step(j, factor):
        factor = factor * time_step / (j + 1).astype(f32)
        slopes_into(x, matrices, s)
        active = jnp.where(degree >= j, factor, 0.0)
        for half in range(2):
            weight = active[:, 128 * half : 128 * (half + 1)]

            def finish(at, lanes, acc):
                kept = -keep[pl.ds(at, 8), lanes]
                for g in range(F):
                    t = acc[g] * kept
                    x[g, pl.ds(at, 8), lanes] = t
                    ahead[g, pl.ds(at, 8), lanes] = ahead[g, pl.ds(at, 8), lanes] + weight * t

            apply_jacobian(s, a, half, jnp.where(j <= top[half], blocks[half], 0), finish)
        return factor

    lax.fori_loop(1, 7, step, jnp.float32(time_step))
    for f in range(F):
        hi, lo = split(ahead[f])
        ahead_ref[f] = (dot(hi, spread) + dot(lo, spread))[0:M]


def call(kernel, outs, scratch, smem, args, flops, limit=24):
    specs = [pl.BlockSpec(memory_space=pltpu.SMEM if i < smem else pltpu.VMEM) for i in range(len(args))]
    return pl.pallas_call(
        kernel,
        out_shape=[jax.ShapeDtypeStruct(o, f32) for o in outs],
        in_specs=specs,
        out_specs=[pl.BlockSpec(memory_space=pltpu.VMEM) for _ in outs],
        scratch_shapes=[pltpu.VMEM(shape, kind) for shape, kind in scratch],
        compiler_params=pltpu.CompilerParams(vmem_limit_bytes=limit * 1024 * 1024),
        cost_estimate=pl.CostEstimate(flops=flops, bytes_accessed=4000000, transcendentals=0),
    )(*args)


def ring(count, step):
    return [(i, (i + step) % count) for i in range(count)]


def shards(
    state, predictor, degree, material, face_link, publish, new_owner, new_index, derivative, trace_ops, lift_ops,
    jacobians, speeds, normals,
):
    me = lax.axis_index("narrow").astype(jnp.int32).reshape(1)
    row = lambda v: v.reshape(1, E)
    published = jnp.concatenate([publish, jnp.full((8,), -1, jnp.int32)]).reshape(16, 1)
    (mine,) = call(pick_kernel, [(8, PICK + JROWS)], [], 0, [predictor, row(degree), published, jnp.transpose(jacobians, (1, 2, 0, 3)), speeds.reshape(8, 1)], 10**9)
    shared = jnp.concatenate([mine] + [lax.ppermute(mine, "narrow", ring(4, s)) for s in (1, 2, 3)], axis=0)
    picks, jac = shared[:, :PICK], shared[:, PICK:]
    low = lax.ppermute(picks, "dom", ring(128, 1))
    high = lax.ppermute(picks, "dom", ring(128, -1))
    own, near = call(
        trace_kernel,
        [(4, F * QP, E), (4, F * QP, E)],
        [((128, 128), f32), ((2 * F * QP, 4 * E), bf16)],
        0,
        [predictor, row(degree), trace_ops, face_link],
        4 * 10**9,
    )
    base, a = call(
        local_kernel,
        [(F, MP, E), (JROWS, E)],
        [((F, MP, E), f32), ((F, 272, E), f32), ((272, 128), f32)],
        1,
        [me, state, predictor, row(degree), row(material), jac, derivative],
        4 * 10**9,
    )
    around = jnp.concatenate([low, picks, high, jnp.zeros((32, PICK), f32)], axis=0)
    (outgoing,) = call(
        flux_kernel,
        [(128, 4, PAY)],
        [
            ((128, 128), f32),
            ((F * QP, 512), f32),
            ((4, F * QP, E), f32),
            ((96, 128), f32),
            ((4, AR, E), f32),
            ((F, 128, E), f32),
            ((PAY, E), f32),
        ],
        1,
        [me, own, near, base, a, around, face_link, normals, trace_ops, lift_ops, row(degree), row(material),
         row(new_owner), new_owner.reshape(E, 1), row(new_index)],
        4 * 10**9,
    )
    arrived = lax.all_to_all(outgoing, "dom", split_axis=0, concat_axis=0, tiled=True)
    corrected, ahead = call(
        predict_kernel,
        [(F, M, E), (F, M, E)],
        [
            ((PAY, E), f32),
            ((E, PAY), f32),
            ((F, MP, E), f32),
            ((F, 272, E), f32),
            ((JROWS, E), f32),
            ((272, 128), f32),
            ((MP, E), f32),
            ((F, MP, E), f32),
        ],
        1,
        [me, arrived, jac, derivative],
        10**10,
    )
    return corrected, ahead


def solution(mesh):
    both = ("dom", "narrow")
    placed = (
        P(None, None, both), P(None, None, both), P(both), P(both), P(None, both), P(both), P(both), P(both),
        P(), P(), P(), P("narrow", None, None, None), P("narrow"), P(None, None, both),
    )
    return jax.shard_map(
        shards,
        mesh=mesh,
        in_specs=placed,
        out_specs=(P(None, None, both), P(None, None, both)),
        check_vma=False,
    )
```

profile of v0, /device:TPU:1, one launch (start us, length us, event | category | flops | bytes accessed | tf_op | source)
XLA Modules:
  0.0 189.6 jit_solution(10931617840579735485)
XLA Ops:
  0.6 0.7 pad_bitcast_fusion
  1.3 0.7 copy.23.speed_ref
  2.0 0.1 copy.22.publish_ref
  2.1 1.3 copy-done.1
  3.4 0.9 copy-done.4
  4.3 0.7 copy-done.8
  5.0 0.5 shard_map.150
  5.5 5.5 %collective-permute-start.2 = (f32[8,2304]{1,0:T(8,128)S(1)}, f32[8,2304]{1,0:T(8,128)S(1)}, u32[]{:S(2)}, u32[]{:S(2)}) collective-permute-start(f32[8,2304]{1,0:T(8,128)S(1)} %shard_map.150), channel_id=1, source_target_pairs={{0,3},{1,0},{2,1},{3,2},{4,7},{5,4},{6,5},{7,6},{8,11},{9,8},{10,9... | collective-permute-start | bytes 221192 | tf_op jit(solution)/shard_map/ppermute | solution.py:322
  10.9 2.3 %collective-permute-start.1 = (f32[8,2304]{1,0:T(8,128)S(1)}, f32[8,2304]{1,0:T(8,128)S(1)}, u32[]{:S(2)}, u32[]{:S(2)}) collective-permute-start(f32[8,2304]{1,0:T(8,128)S(1)} %shard_map.150), channel_id=1, source_target_pairs={{0,2},{1,3},{2,0},{3,1},{4,6},{5,7},{6,4},{7,5},{8,10},{9,11},{10,... | collective-permute-start | bytes 221192 | tf_op jit(solution)/shard_map/ppermute | solution.py:322
  13.2 2.6 %collective-permute-start = (f32[8,2304]{1,0:T(8,128)S(1)}, f32[8,2304]{1,0:T(8,128)S(1)}, u32[]{:S(2)}, u32[]{:S(2)}) collective-permute-start(f32[8,2304]{1,0:T(8,128)S(1)} %shard_map.150), channel_id=1, source_target_pairs={{0,1},{1,2},{2,3},{3,0},{4,5},{5,6},{6,7},{7,4},{8,9},{9,10},{10,1... | collective-permute-start | bytes 221192 | tf_op jit(solution)/shard_map/ppermute | solution.py:322
  15.9 2.5 %shard_map.149 = (f32[4,416,256]{2,1,0:T(8,128)S(1)}, f32[4,416,256]{2,1,0:T(8,128)S(1)}) custom-call(f32[13,84,256]{2,1,0:T(8,128)S(1)} %copy-done.1, s32[1,256]{1,0:T(1,128)S(1)} %bitcast.14, f32[4,28,84]{2,1,0:T(8,128)S(1)} %copy.21.trace_ref, s32[4,256]{1,0:T(4,128)S(1)} %copy-done.7), custom_call_target="tpu_custom_call" | custom-call | flops 4000000000 | bytes 4000000 | tf_op jit(solution)/shard_map/pallas_call | solution.py:299
  18.4 1.2 copy-done.12
  19.7 1.2 copy-done.14
  20.8 0.1 copy.26.owner_col_ref
  21.0 0.1 copy.25.lift_ref
  21.1 0.1 pad.4.clone
  21.3 6.2 %collective-permute-start.4 = (f32[32,1664]{1,0:T(8,128)S(1)}, f32[32,1664]{1,0:T(8,128)S(1)}, u32[]{:S(2)}, u32[]{:S(2)}) collective-permute-start(f32[32,1664]{1,0:T(8,128)S(1)} %pad_maximum_fusion), channel_id=1, source_target_pairs={{0,508},{4,0},{8,4},{12,8},{16,12},{20,16},{24,20},{28,24},{32,28}... | collective-permute-start | bytes 638984 | tf_op jit(solution)/shard_map/ppermute | solution.py:325
  27.5 1.9 %collective-permute-start.3 = (f32[32,1664]{1,0:T(8,128)S(1)}, f32[32,1664]{1,0:T(8,128)S(1)}, u32[]{:S(2)}, u32[]{:S(2)}) collective-permute-start(f32[32,1664]{1,0:T(8,128)S(1)} %pad_maximum_fusion), channel_id=1, source_target_pairs={{0,4},{4,8},{8,12},{12,16},{16,20},{20,24},{24,28},{28,32},{32,36}... | collective-permute-start | bytes 638984 | tf_op jit(solution)/shard_map/ppermute | solution.py:324
  29.5 4.5 %shard_map.151 = (f32[13,96,256]{2,1,0:T(8,128)S(1)}, f32[640,256]{1,0:T(8,128)S(1)}) custom-call(s32[1]{0:T(128)} %bitcast.me_ref, f32[13,84,256]{2,1,0:T(8,128)S(1)} %copy-done.3, f32[13,84,256]{2,1,0:T(8,128)S(1)} %copy-done.2, s32[1,256]{1,0:T(1,128)S(1)} %bitcast.15, s32[1,256]{1,0:T(1,128)S(1)} %bitcast.17, f32[32,640]{1,0:T(8,128)S(1)} %pad_maximum_fusion.3.jac_ref, ...), custom_call_target="tpu_custom_call" | custom-call | flops 4000000000 | bytes 4000000 | tf_op jit(solution)/shard_map/pallas_call | solution.py:299
  34.0 3.8 %collective-permute-done.3 = f32[32,1664]{1,0:T(8,128)S(1)} collective-permute-done((f32[32,1664]{1,0:T(8,128)S(1)}, f32[32,1664]{1,0:T(8,128)S(1)}, u32[]{:S(2)}, u32[]{:S(2)}) %collective-permute-start.3) | collective-permute-done | bytes 213024 | tf_op jit(solution)/shard_map/ppermute | solution.py:324
  37.8 0.1 maximum_maximum_fusion.pick_ref
  38.0 5.8 %shard_map.152 = f32[128,4,1152]{2,1,0:T(4,128)S(1)} custom-call(s32[1]{0:T(128)} %bitcast.me_ref, f32[4,416,256]{2,1,0:T(8,128)S(1)} %copy-done.13, f32[4,416,256]{2,1,0:T(8,128)S(1)} %copy-done.15, f32[13,96,256]{2,1,0:T(8,128)S(1)} %get-tuple-element.8.base_ref, f32[640,256]{1,0:T(8,128)S(1)} %get-tuple-element.9.a_ref, ...), custom_call_target="tpu_custom_call" | custom-call | flops 4000000000 | bytes 4000000 | tf_op jit(solution)/shard_map/pallas_call | solution.py:299
  43.8 122.7 %all_to_all.5.arrived_ref = f32[128,4,1152]{2,1,0:T(4,128)S(1)} all-to-all(f32[128,4,1152]{2,1,0:T(4,128)S(1)} %shard_map.152), channel_id=1, replica_groups=mesh['dom'=128,'narrow'=4] {'dom'}, dimensions={0} | all-to-all | bytes 4718592 | tf_op jit(solution)/shard_map/all_to_all | solution.py:360
  166.5 23.1 %shard_map.153 = (f32[13,84,256]{2,1,0:T(8,128)}, f32[13,84,256]{2,1,0:T(8,128)}) custom-call(s32[1]{0:T(128)} %bitcast.me_ref, f32[128,4,1152]{2,1,0:T(4,128)S(1)} %all_to_all.5.arrived_ref, f32[32,640]{1,0:T(8,128)S(1)} %pad_maximum_fusion.3.jac_ref, f32[3,84,84]{2,1,0:T(8,128)S(1)} %copy-done.5), custom_call_target="tpu_custom_call" | custom-call | flops 10000000000 | bytes 4000000 | tf_op jit(solution)/shard_map/pallas_call | solution.py:299
  (39 shorter events, 0.1 us)
Async XLA Ops:
  2.1 1.3 copy-start.1
  3.4 0.9 copy-start.4
  4.3 0.7 copy-start.8
  5.0 10.8 %copy-start.16 = (f32[4,28,84]{2,0,1:T(4,128)S(1)}, f32[4,28,84]{2,0,1:T(4,128)}, u32[]{:S(2)}) copy-start(f32[4,28,84]{2,0,1:T(4,128)} %param.23) | copy-start | bytes 112900
  5.0 10.9 %copy-start.7 = (s32[4,256]{1,0:T(4,128)S(1)}, s32[4,256]{1,0:T(4,128)}, u32[]{:S(2)}) copy-start(s32[4,256]{1,0:T(4,128)} %link_ref.3) | copy-start | bytes 12292
  5.5 15.8 %collective-permute-start.2 = (f32[8,2304]{1,0:T(8,128)S(1)}, f32[8,2304]{1,0:T(8,128)S(1)}, u32[]{:S(2)}, u32[]{:S(2)}) collective-permute-start(f32[8,2304]{1,0:T(8,128)S(1)} %shard_map.150), channel_id=1, source_target_pairs={{0,3},{1,0},{2,1},{3,2},{4,7},{5,4},{6,5},{7,6},{8,11},{9,8},{10,9... | collective-permute-start | bytes 221192 | tf_op jit(solution)/shard_map/ppermute | solution.py:322
  10.9 10.3 %collective-permute-start.1 = (f32[8,2304]{1,0:T(8,128)S(1)}, f32[8,2304]{1,0:T(8,128)S(1)}, u32[]{:S(2)}, u32[]{:S(2)}) collective-permute-start(f32[8,2304]{1,0:T(8,128)S(1)} %shard_map.150), channel_id=1, source_target_pairs={{0,2},{1,3},{2,0},{3,1},{4,6},{5,7},{6,4},{7,5},{8,10},{9,11},{10,... | collective-permute-start | bytes 221192 | tf_op jit(solution)/shard_map/ppermute | solution.py:322
  13.2 8.0 %collective-permute-start = (f32[8,2304]{1,0:T(8,128)S(1)}, f32[8,2304]{1,0:T(8,128)S(1)}, u32[]{:S(2)}, u32[]{:S(2)}) collective-permute-start(f32[8,2304]{1,0:T(8,128)S(1)} %shard_map.150), channel_id=1, source_target_pairs={{0,1},{1,2},{2,3},{3,0},{4,5},{5,6},{6,7},{7,4},{8,9},{9,10},{10,1... | collective-permute-start | bytes 221192 | tf_op jit(solution)/shard_map/ppermute | solution.py:322
  15.8 5.0 %copy-start = (s32[256]{0:T(256)S(1)}, s32[256]{0:T(256)}, u32[]{:S(2)}) copy-start(s32[256]{0:T(256)} %param.20) | copy-start | bytes 3076
  15.9 5.1 %copy-start.17 = (f32[4,84,28]{1,0,2:T(4,128)S(1)}, f32[4,84,28]{1,0,2:T(4,128)}, u32[]{:S(2)}) copy-start(f32[4,84,28]{1,0,2:T(4,128)} %param.24) | copy-start | bytes 112900
  15.9 13.6 %copy-start.2 = (f32[13,84,256]{2,1,0:T(8,128)S(1)}, f32[13,84,256]{2,1,0:T(8,128)}, u32[]{:S(2)}) copy-start(f32[13,84,256]{2,1,0:T(8,128)} %pred_ref.5) | copy-start | bytes 3354628
  15.9 13.6 %copy-start.3 = (f32[13,84,256]{2,1,0:T(8,128)S(1)}, f32[13,84,256]{2,1,0:T(8,128)}, u32[]{:S(2)}) copy-start(f32[13,84,256]{2,1,0:T(8,128)} %state_ref.1) | copy-start | bytes 3354628
  15.9 13.6 %copy-start.5 = (f32[3,84,84]{2,1,0:T(8,128)S(1)}, f32[3,84,84]{2,1,0:T(8,128)}, u32[]{:S(2)}) copy-start(f32[3,84,84]{2,1,0:T(8,128)} %der_ref.3) | copy-start | bytes 254020
  15.9 13.6 %copy-start.9 = (s32[256]{0:T(256)S(1)}, s32[256]{0:T(256)}, u32[]{:S(2)}) copy-start(s32[256]{0:T(256)} %param.16) | copy-start | bytes 3076
  15.9 13.6 %copy-start.10 = (s32[256]{0:T(256)S(1)}, s32[256]{0:T(256)}, u32[]{:S(2)}) copy-start(s32[256]{0:T(256)} %param.17) | copy-start | bytes 3076
  18.4 1.2 copy-start.12
  19.7 1.2 copy-start.14
  21.3 12.8 %collective-permute-start.4 = (f32[32,1664]{1,0:T(8,128)S(1)}, f32[32,1664]{1,0:T(8,128)S(1)}, u32[]{:S(2)}, u32[]{:S(2)}) collective-permute-start(f32[32,1664]{1,0:T(8,128)S(1)} %pad_maximum_fusion), channel_id=1, source_target_pairs={{0,508},{4,0},{8,4},{12,8},{16,12},{20,16},{24,20},{28,24},{32,28}... | collective-permute-start | bytes 638984 | tf_op jit(solution)/shard_map/ppermute | solution.py:325
  27.5 10.4 %collective-permute-start.3 = (f32[32,1664]{1,0:T(8,128)S(1)}, f32[32,1664]{1,0:T(8,128)S(1)}, u32[]{:S(2)}, u32[]{:S(2)}) collective-permute-start(f32[32,1664]{1,0:T(8,128)S(1)} %pad_maximum_fusion), channel_id=1, source_target_pairs={{0,4},{4,8},{8,12},{12,16},{16,20},{20,24},{24,28},{28,32},{32,36}... | collective-permute-start | bytes 638984 | tf_op jit(solution)/shard_map/ppermute | solution.py:324
  29.5 8.5 %copy-start.13 = (f32[4,416,256]{2,1,0:T(8,128)S(1)}, f32[4,416,256]{2,1,0:T(8,128)}, u32[]{:S(2)}) copy-start(f32[4,416,256]{2,1,0:T(8,128)} %copy-done.12) | copy-start | bytes 5111812
  29.5 8.5 %copy-start.15 = (f32[4,416,256]{2,1,0:T(8,128)S(1)}, f32[4,416,256]{2,1,0:T(8,128)}, u32[]{:S(2)}) copy-start(f32[4,416,256]{2,1,0:T(8,128)} %copy-done.14) | copy-start | bytes 5111812
  34.0 4.0 %copy-start.6 = (f32[3,4,256]{2,1,0:T(4,128)S(1)}, f32[3,4,256]{2,1,0:T(4,128)}, u32[]{:S(2)}) copy-start(f32[3,4,256]{2,1,0:T(4,128)} %normals_ref.1) | copy-start | bytes 36868
  34.0 4.0 %copy-start.11 = (s32[256]{0:T(256)S(1)}, s32[256]{0:T(256)}, u32[]{:S(2)}) copy-start(s32[256]{0:T(256)} %param.21) | copy-start | bytes 3076
where the time goes:
time: 191 us; the launch traced here: 190 us
  blocking collectives  123 us (64%)
  Pallas kernels  36.3 us (19%)
  starting transfers between devices  18.5 us (10%)
  local copies, waits for them, and re-layouts  7.16 us (4%)
  waiting for transfers between devices  3.83 us (2%)
    all_to_all x1, blocking collectives, shards(): lax.all_to_all(outgoing, 'dom', split_axis=0, concat_axis=0, tiled=True)  123 us
    pallas_call x5, Pallas kernels, call(): pl.pallas_call(kernel, out_shape=[jax.ShapeDtypeStruct(o, f32) for o in o...  36.3 us
    ppermute x3, starting transfers between devices, shards(): lax.ppermute(mine, 'narrow', ring(4, s))  10.3 us
    ppermute x1, starting transfers between devices, shards(): high = lax.ppermute(picks, 'dom', ring(128, -1))  6.22 us
    unnamed x38, local copies, waits for them, and re-layouts  5.48 us
  transfers between devices with their start and end apart: 5, of which 1 were waited for; matrix products, arithmetic and copies ran while one was open for 0% of the time, Pallas kernels for 4%

commit v1 on v0

--- a/solution.py
+++ b/solution.py
@@ -16,6 +16,7 @@
 AR = 176
 SLOTS = 512
 PAY = 1152
+FORWARD = 64
 INFO = F * MS
 PICK = F * 128
 JROWS = 640
@@ -103,8 +104,11 @@
 
 def pick_kernel(pred_ref, degree_ref, publish_ref, jac_ref, speed_ref, out_ref):
     keep = keep_rows(degree_ref[...], M)
+    eye = lax.broadcasted_iota(jnp.int32, (8, 8), 0) == lax.broadcasted_iota(jnp.int32, (8, 8), 1)
+    column = lambda v: jnp.sum(jnp.where(eye, v, 0.0), axis=1, keepdims=True)
+    published = pad_rows(column(publish_ref[...].astype(f32)), 16).astype(jnp.int32)
     e = lax.broadcasted_iota(jnp.int32, (16, E), 1)
-    onehot = (e == publish_ref[...]).astype(f32).astype(bf16)
+    onehot = (e == published).astype(f32).astype(bf16)
     out_ref[...] = jnp.zeros(out_ref.shape, f32)
     for f in range(F):
         hi, lo = split(pred_ref[f] * keep)
@@ -114,7 +118,7 @@
         for g in range(F):
             at = PICK + d * AR + g * F
             out_ref[:, at : at + F] = jac_ref[d, g]
-    out_ref[:, PICK + 3 * AR : PICK + 3 * AR + 1] = speed_ref[...]
+    out_ref[:, PICK + 3 * AR : PICK + 3 * AR + 1] = column(speed_ref[...])
 
 
 def trace_matrix(trace_ref, scr):
@@ -173,7 +177,7 @@
 
 def flux_kernel(
     me_ref, own_ref, near_ref, base_ref, a_ref, pick_ref, link_ref, normals_ref, trace_ref, lift_ref, degree_ref, material_ref,
-    owner_row_ref, owner_col_ref, index_ref, out_ref, tscr, far, outside, lscr, dirs, flux, u,
+    owner_row_ref, owner_col_ref, index_ref, out_ref, u, tscr, far, outside, lscr, dirs, flux,
 ):
     me = me_ref[0]
     thi, tlo = trace_matrix(trace_ref, tscr)
@@ -228,25 +232,73 @@
         lifted = dot(lhh, jnp.concatenate([hi, lo], axis=0)) + dot(llo, hi)
         u[f * MS : (f + 1) * MS, :] = (base_ref[f, 0:MS, :] - lifted[0:MS]) * keep
     u[INFO : INFO + 8, :] = jnp.concatenate(
-        [degree_ref[...], material_ref[...], index_ref[...] + 1, jnp.zeros((5, E), jnp.int32)], axis=0
+        [degree_ref[...], material_ref[...], index_ref[...] + 1, owner_row_ref[...] % 2, jnp.zeros((4, E), jnp.int32)], axis=0
     ).astype(f32)
-    owner = owner_row_ref[...]
+    owner, other = owner_row_ref[...], owner_col_ref[...]
+    rank = ranks(owner, other)
+    full = jnp.max(jnp.sum(jnp.where(other // 2 == owner // 2, 1.0, 0.0), axis=0, keepdims=True))
+    at = jnp.where(owner % 2 == 0, rank, 5 - rank)
+    target, slot = owner // 2 * 2 + at // 3, at % 3
+    dest = lax.broadcasted_iota(jnp.int32, (128, E), 0)
+    flag = jnp.where(lax.broadcasted_iota(jnp.int32, (128, 384), 1) == INFO + 4 - 768, jnp.where(full > 6.0, 1.0, 0.0), 0.0)
+    for c in range(3):
+        hi, lo = split(u[c * 384 : (c + 1) * 384, :])
+        for j in range(3):
+            pick = ((dest == target) & (slot == j)).astype(f32).astype(bf16)
+            got = dot(pick, hi, NT) + dot(pick, lo, NT)
+            out_ref[:, 0, j * PAY + c * 384 : j * PAY + (c + 1) * 384] = got + flag if c == 2 and j == 0 else got
+
+
+def ranks(owner_row, owner_col):
     before = lax.broadcasted_iota(jnp.int32, (E, E), 0) < lax.broadcasted_iota(jnp.int32, (E, E), 1)
-    rank = jnp.sum(jnp.where((owner_col_ref[...] == owner) & before, 1.0, 0.0), axis=0, keepdims=True)
-    slot = owner * 4 + rank.astype(jnp.int32)
+    return jnp.sum(jnp.where((owner_col == owner_row) & before, 1.0, 0.0), axis=0, keepdims=True).astype(jnp.int32)
+
+
+def slot_kernel(u_ref, owner_row_ref, owner_col_ref, out_ref):
+    slot = owner_row_ref[...] * 4 + ranks(owner_row_ref[...], owner_col_ref[...])
     pick = (lax.broadcasted_iota(jnp.int32, (SLOTS, E), 0) == slot).astype(f32).astype(bf16)
     for c in range(3):
-        hi, lo = split(u[c * 384 : (c + 1) * 384, :])
-        out_ref[:, :, c * 384 : (c + 1) * 384] = (dot(pick, hi, NT) + dot(pick, lo, NT)).reshape(SLOTS // 4, 4, 384)
-
-
-def predict_kernel(me_ref, arrived_ref, jac_ref, der_ref, corrected_ref, ahead_ref, c, r, x, s, a, dscr, keep, ahead):
-    arrived = arrived_ref[...].reshape(SLOTS, PAY)
+        hi, lo = split(u_ref[c * 384 : (c + 1) * 384, :])
+        out_ref[:, c * 384 : (c + 1) * 384] = dot(pick, hi, NT) + dot(pick, lo, NT)
+
+
+def forward_kernel(core_ref, arrived_ref, out_ref, flag_ref):
+    tail = jnp.concatenate([arrived_ref[:, 0, j * PAY + PAY - 128 : (j + 1) * PAY] for j in range(3)], axis=0)
+    info = jnp.transpose(tail)
+    at = INFO - (PAY - 128)
+    foreign = (info[at : at + 1] > 0) & (info[at + 3 : at + 4] != core_ref[0].astype(f32))
+    here = jnp.where(foreign, 1.0, 0.0)
+    before = lax.broadcasted_iota(jnp.int32, (384, 384), 0) < lax.broadcasted_iota(jnp.int32, (384, 384), 1)
+    count = dot(jnp.broadcast_to(here, (16, 384)).astype(bf16), before.astype(f32).astype(bf16))[0:1].astype(jnp.int32)
+    place = jnp.where(foreign, count, -1)
+    pick = (lax.broadcasted_iota(jnp.int32, (FORWARD, 384), 0) == place).astype(f32).astype(bf16)
+    for c in range(3):
+        part = [arrived_ref[:, 0, j * PAY + c * 384 : j * PAY + (c + 1) * 384] for j in range(3)]
+        hi, lo = split(jnp.concatenate(part, axis=0))
+        out_ref[:, c * 384 : (c + 1) * 384] = dot(pick, hi) + dot(pick, lo)
+    flag_ref[...] = jnp.broadcast_to(jnp.max(info[at + 4 : at + 5], axis=1, keepdims=True), (1, 128))
+
+
+def predict_shared_kernel(me_ref, arrived_ref, forwarded_ref, *refs):
+    records = jnp.concatenate(
+        [arrived_ref[:, 0, j * PAY : (j + 1) * PAY] for j in range(3)] + [forwarded_ref[...], jnp.zeros((SLOTS - 384 - FORWARD, PAY), f32)],
+        axis=0,
+    )
+    predict(me_ref, records, *refs)
+
+
+def predict_kernel(me_ref, arrived_ref, *refs):
+    predict(me_ref, arrived_ref[...], *refs)
+
+
+def predict(me_ref, arrived, jac_ref, der_ref, corrected_ref, ahead_ref, c, r, x, s, a, dscr, keep, ahead):
     info = jnp.transpose(arrived[:, PAY - 128 :])
-    lead = info[INFO - (PAY - 128) : INFO - (PAY - 128) + 1]
+    at = INFO - (PAY - 128)
+    core = me_ref[1].astype(f32)
+    lead = jnp.where(info[at + 3 : at + 4] == core, info[at : at + 1], 0.0)
     slot_row = lax.broadcasted_iota(jnp.int32, (SLOTS, SLOTS), 1)
     slot_col = lax.broadcasted_iota(jnp.int32, (SLOTS, SLOTS), 0)
-    degree_col = arrived[:, INFO : INFO + 1]
+    degree_col = jnp.where(arrived[:, INFO + 3 : INFO + 4] == core, arrived[:, INFO : INFO + 1], 0.0)
     ahead_of = (degree_col > lead) | ((degree_col == lead) & (slot_col < slot_row))
     rank = jnp.sum(jnp.where(ahead_of, 1.0, 0.0), axis=0, keepdims=True)
     rank = jnp.where(lead > 0, rank, -1.0).astype(jnp.int32)
@@ -315,10 +367,10 @@
     state, predictor, degree, material, face_link, publish, new_owner, new_index, derivative, trace_ops, lift_ops,
     jacobians, speeds, normals,
 ):
-    me = lax.axis_index("narrow").astype(jnp.int32).reshape(1)
+    core = lax.axis_index("dom").astype(jnp.int32) % 2
+    me = jnp.stack([lax.axis_index("narrow").astype(jnp.int32), core])
     row = lambda v: v.reshape(1, E)
-    published = jnp.concatenate([publish, jnp.full((8,), -1, jnp.int32)]).reshape(16, 1)
-    (mine,) = call(pick_kernel, [(8, PICK + JROWS)], [], 0, [predictor, row(degree), published, jnp.transpose(jacobians, (1, 2, 0, 3)), speeds.reshape(8, 1)], 10**9)
+    (mine,) = call(pick_kernel, [(8, PICK + JROWS)], [], 0, [predictor, row(degree), publish.reshape(1, 8), jnp.transpose(jacobians, (1, 2, 0, 3)), speeds.reshape(1, 8)], 10**9, 12)
     shared = jnp.concatenate([mine] + [lax.ppermute(mine, "narrow", ring(4, s)) for s in (1, 2, 3)], axis=0)
     picks, jac = shared[:, :PICK], shared[:, PICK:]
     low = lax.ppermute(picks, "dom", ring(128, 1))
@@ -340,9 +392,10 @@
         4 * 10**9,
     )
     around = jnp.concatenate([low, picks, high, jnp.zeros((32, PICK), f32)], axis=0)
-    (outgoing,) = call(
+    owners = [row(new_owner), new_owner.reshape(E, 1)]
+    outgoing, updated = call(
         flux_kernel,
-        [(128, 4, PAY)],
+        [(128, 1, 3 * PAY), (PAY, E)],
         [
             ((128, 128), f32),
             ((F * QP, 512), f32),
@@ -350,31 +403,39 @@
             ((96, 128), f32),
             ((4, AR, E), f32),
             ((F, 128, E), f32),
-            ((PAY, E), f32),
         ],
         1,
         [me, own, near, base, a, around, face_link, normals, trace_ops, lift_ops, row(degree), row(material),
-         row(new_owner), new_owner.reshape(E, 1), row(new_index)],
+         *owners, row(new_index)],
         4 * 10**9,
     )
+    scratch = [
+        ((PAY, E), f32),
+        ((E, PAY), f32),
+        ((F, MP, E), f32),
+        ((F, 272, E), f32),
+        ((JROWS, E), f32),
+        ((272, 128), f32),
+        ((MP, E), f32),
+        ((F, MP, E), f32),
+    ]
     arrived = lax.all_to_all(outgoing, "dom", split_axis=0, concat_axis=0, tiled=True)
-    corrected, ahead = call(
-        predict_kernel,
-        [(F, M, E), (F, M, E)],
-        [
-            ((PAY, E), f32),
-            ((E, PAY), f32),
-            ((F, MP, E), f32),
-            ((F, 272, E), f32),
-            ((JROWS, E), f32),
-            ((272, 128), f32),
-            ((MP, E), f32),
-            ((F, MP, E), f32),
-        ],
-        1,
-        [me, arrived, jac, derivative],
-        10**10,
-    )
+    forwarded, flag = call(forward_kernel, [(FORWARD, PAY), (1, 128)], [], 1, [core.reshape(1), arrived], 10**8, 16)
+    forwarded = lax.ppermute(forwarded, "dom", [(i, i ^ 1) for i in range(128)])
+
+    def shared(arrived, forwarded, updated, jac, derivative, *rest):
+        return tuple(call(
+            predict_shared_kernel, [(F, M, E), (F, M, E)], scratch, 1, [me, arrived, forwarded, jac, derivative], 10**10
+        ))
+
+    def apart(arrived, forwarded, updated, jac, derivative, *rest):
+        (slots,) = call(slot_kernel, [(SLOTS, PAY)], [], 0, [updated, *rest], 10**9)
+        slots = lax.all_to_all(slots.reshape(128, 4, PAY), "dom", split_axis=0, concat_axis=0, tiled=True)
+        return tuple(call(
+            predict_kernel, [(F, M, E), (F, M, E)], scratch, 1, [me, slots.reshape(SLOTS, PAY), jac, derivative], 10**10
+        ))
+
+    corrected, ahead = lax.cond(flag[0, 0] > 0, apart, shared, arrived, forwarded, updated, jac, derivative, *owners)
     return corrected, ahead
 
 

time: 191 us -> 172 us (0.901)
  blocking collectives: 123 us -> 97.2 us
  starting transfers between devices: 18.5 us -> 25 us
  Pallas kernels: 36.3 us -> 39.7 us
  local copies, waits for them, and re-layouts: 7.16 us -> 4.57 us
    all_to_all x1, blocking collectives: 123 us -> 97.2 us  [shards(): lax.all_to_all(outgoing, 'dom', split_axis=0, concat_axis=0, tiled=True)]
    ppermute x0 -> x1, starting transfers between devices: none -> 5.27 us  [shards(): forwarded = lax.ppermute(forwarded, 'dom', [(i, i ^ 1) for i in range(128)])]
    pallas_call x5 -> x6, Pallas kernels: 36.3 us -> 39.7 us  [call(): pl.pallas_call(kernel, out_shape=[jax.ShapeDtypeStruct(o, f32) for o in o...]
    unnamed x38 -> x34, local copies, waits for them, and re-layouts: 5.48 us -> 4.36 us
  transfers between devices with their start and end apart: 5 -> 6, of which waited for: 1 -> 3; matrix products, arithmetic and copies ran while one was open for 0% -> 0% of each run, Pallas kernels for 4% -> 4%
where the time goes in v1:
time: 172 us
  blocking collectives  97.2 us (57%)
  Pallas kernels  39.7 us (23%)
  starting transfers between devices  25 us (15%)
  local copies, waits for them, and re-layouts  4.57 us (3%)
  waiting for transfers between devices  4.11 us (2%)
    all_to_all x1, blocking collectives, shards(): lax.all_to_all(outgoing, 'dom', split_axis=0, concat_axis=0, tiled=True)  97.2 us
    pallas_call x6, Pallas kernels, call(): pl.pallas_call(kernel, out_shape=[jax.ShapeDtypeStruct(o, f32) for o in o...  39.7 us
    ppermute x3, starting transfers between devices, shards(): lax.ppermute(mine, 'narrow', ring(4, s))  10.3 us
    ppermute x1, starting transfers between devices, shards(): high = lax.ppermute(picks, 'dom', ring(128, -1))  7.5 us
    ppermute x1, starting transfers between devices, shards(): forwarded = lax.ppermute(forwarded, 'dom', [(i, i ^ 1) for i in range(128)])  5.27 us
    unnamed x34, local copies, waits for them, and re-layouts  4.36 us
  transfers between devices with their start and end apart: 6, of which 3 were waited for; matrix products, arithmetic and copies ran while one was open for 0% of the time, Pallas kernels for 4%

profile of v1, /device:TPU:1, one launch (start us, length us, event | category | flops | bytes accessed | tf_op | source)
XLA Modules:
  0.0 171.7 jit_solution(11600198420739808562)
XLA Ops:
  0.6 1.3 copy-done
  1.9 0.9 copy-done.3
  2.8 0.7 copy-done.6
  3.5 0.7 copy-done.10
  4.2 0.7 copy-done.11
  4.8 0.6 shard_map.154
  5.4 5.5 %collective-permute-start.2 = (f32[8,2304]{1,0:T(8,128)S(1)}, f32[8,2304]{1,0:T(8,128)S(1)}, u32[]{:S(2)}, u32[]{:S(2)}) collective-permute-start(f32[8,2304]{1,0:T(8,128)S(1)} %shard_map.154), channel_id=1, source_target_pairs={{0,3},{1,0},{2,1},{3,2},{4,7},{5,4},{6,5},{7,6},{8,11},{9,8},{10,9... | collective-permute-start | bytes 221192 | tf_op jit(solution)/shard_map/ppermute | solution.py:374
  10.9 2.3 %collective-permute-start.1 = (f32[8,2304]{1,0:T(8,128)S(1)}, f32[8,2304]{1,0:T(8,128)S(1)}, u32[]{:S(2)}, u32[]{:S(2)}) collective-permute-start(f32[8,2304]{1,0:T(8,128)S(1)} %shard_map.154), channel_id=1, source_target_pairs={{0,2},{1,3},{2,0},{3,1},{4,6},{5,7},{6,4},{7,5},{8,10},{9,11},{10,... | collective-permute-start | bytes 221192 | tf_op jit(solution)/shard_map/ppermute | solution.py:374
  13.2 2.6 %collective-permute-start = (f32[8,2304]{1,0:T(8,128)S(1)}, f32[8,2304]{1,0:T(8,128)S(1)}, u32[]{:S(2)}, u32[]{:S(2)}) collective-permute-start(f32[8,2304]{1,0:T(8,128)S(1)} %shard_map.154), channel_id=1, source_target_pairs={{0,1},{1,2},{2,3},{3,0},{4,5},{5,6},{6,7},{7,4},{8,9},{9,10},{10,1... | collective-permute-start | bytes 221192 | tf_op jit(solution)/shard_map/ppermute | solution.py:374
  15.8 0.1 copy.26.owner_col_ref
  16.0 0.1 copy.25.lift_ref
  16.2 2.5 %shard_map.153 = (f32[4,416,256]{2,1,0:T(8,128)S(1)}, f32[4,416,256]{2,1,0:T(8,128)S(1)}) custom-call(f32[13,84,256]{2,1,0:T(8,128)S(1)} %copy-done.1, s32[1,256]{1,0:T(1,128)S(1)} %bitcast.14, f32[4,28,84]{2,1,0:T(8,128)S(1)} %copy.23.trace_ref, s32[4,256]{1,0:T(4,128)S(1)} %copy-done.5), custom_call_target="tpu_custom_call" | custom-call | flops 4000000000 | bytes 4000000 | tf_op jit(solution)/shard_map/pallas_call | solution.py:351
  18.8 0.6 collective-permute-done
  19.5 7.5 %collective-permute-start.4 = (f32[32,1664]{1,0:T(8,128)S(1)}, f32[32,1664]{1,0:T(8,128)S(1)}, u32[]{:S(2)}, u32[]{:S(2)}) collective-permute-start(f32[32,1664]{1,0:T(8,128)S(1)} %pad_maximum_fusion), channel_id=1, source_target_pairs={{0,508},{4,0},{8,4},{12,8},{16,12},{20,16},{24,20},{28,24},{32,28}... | collective-permute-start | bytes 638984 | tf_op jit(solution)/shard_map/ppermute | solution.py:377
  27.0 1.9 %collective-permute-start.3 = (f32[32,1664]{1,0:T(8,128)S(1)}, f32[32,1664]{1,0:T(8,128)S(1)}, u32[]{:S(2)}, u32[]{:S(2)}) collective-permute-start(f32[32,1664]{1,0:T(8,128)S(1)} %pad_maximum_fusion), channel_id=1, source_target_pairs={{0,4},{4,8},{8,12},{12,16},{16,20},{20,24},{24,28},{28,32},{32,36}... | collective-permute-start | bytes 638984 | tf_op jit(solution)/shard_map/ppermute | solution.py:376
  29.0 5.0 %shard_map.155 = (f32[13,96,256]{2,1,0:T(8,128)S(1)}, f32[640,256]{1,0:T(8,128)S(1)}) custom-call(s32[2]{0:T(128)S(1)} %pad_add_fusion.me_ref, f32[13,84,256]{2,1,0:T(8,128)S(1)} %copy-done.2, f32[13,84,256]{2,1,0:T(8,128)S(1)} %copy-done.1, s32[1,256]{1,0:T(1,128)S(1)} %bitcast.15, s32[1,256]{1,0:T(1,128)S(1)} %bitcast.17, ...), custom_call_target="tpu_custom_call" | custom-call | flops 4000000000 | bytes 4000000 | tf_op jit(solution)/shard_map/pallas_call | solution.py:351
  34.0 2.3 %collective-permute-done.3 = f32[32,1664]{1,0:T(8,128)S(1)} collective-permute-done((f32[32,1664]{1,0:T(8,128)S(1)}, f32[32,1664]{1,0:T(8,128)S(1)}, u32[]{:S(2)}, u32[]{:S(2)}) %collective-permute-start.3) | collective-permute-done | bytes 213024 | tf_op jit(solution)/shard_map/ppermute | solution.py:376
  36.5 6.7 %shard_map.156 = (f32[128,1,3456]{2,1,0:T(1,128)S(1)}, f32[1152,256]{1,0:T(8,128)}) custom-call(s32[2]{0:T(128)S(1)} %pad_add_fusion.me_ref, f32[4,416,256]{2,1,0:T(8,128)S(1)} %get-tuple-element.43.own_ref, f32[4,416,256]{2,1,0:T(8,128)S(1)} %get-tuple-element.44.near_ref, f32[13,96,256]{2,1,0:T(8,128)S(1)} %get-tuple-element.45.base_ref, ...), custom_call_target="tpu_custom_call" | custom-call | flops 4000000000 | bytes 4000000 | tf_op jit(solution)/shard_map/pallas_call | solution.py:351
  43.2 97.2 %all_to_all.10.arrived_ref = f32[128,1,3456]{2,1,0:T(1,128)S(1)} all-to-all(f32[128,1,3456]{2,1,0:T(1,128)S(1)} %get-tuple-element.47), channel_id=1, replica_groups=mesh['dom'=128,'narrow'=4] {'dom'}, dimensions={0} | all-to-all | bytes 3538944 | tf_op jit(solution)/shard_map/all_to_all | solution.py:422
  140.4 0.9 shard_map.157
  141.3 5.3 %collective-permute-start.5 = (f32[64,1152]{1,0:T(8,128)S(1)}, f32[64,1152]{1,0:T(8,128)S(1)}, u32[]{:S(2)}, u32[]{:S(2)}) collective-permute-start(f32[64,1152]{1,0:T(8,128)S(1)} %get-tuple-element.49), channel_id=1, source_target_pairs={{0,4},{4,0},{8,12},{12,8},{16,20},{20,16},{24,28},{28,24},{32,36},... | collective-permute-start | bytes 884744 | tf_op jit(solution)/shard_map/ppermute | solution.py:424
  146.6 1.2 collective-permute-done.5
  147.8 23.9 %conditional.1 = ((f32[13,84,256]{2,1,0:T(8,128)}, f32[13,84,256]{2,1,0:T(8,128)})) conditional(s32[]{:T(128)} %bitcast.10, (s32[2]{0:T(128)S(1)}, f32[128,1,3456]{2,1,0:T(1,128)S(1)}, f32[64,1152]{1,0:T(8,128)S(1)}, f32[32,640]{1,0:T(8,128)S(1)}, f32[3,84,84]{2,1,0:T(8,128)S(1)}) %tuple.26, (f32[1152,256]{1,0:T(8,128)}, s32[1,256]{1,0:T(1,128)S(1)}, ...), branch_computations={%region_0.1_spmd, %region_1.2_spmd} | conditional | flops 11000000512 | bytes 22157832 | solution.py:438
  147.8 23.9 %branch_0_fun.1 = (f32[13,84,256]{2,1,0:T(8,128)}, f32[13,84,256]{2,1,0:T(8,128)}) custom-call(s32[2]{0:T(128)S(1)} %get-tuple-element.22.me_ref, f32[128,1,3456]{2,1,0:T(1,128)S(1)} %get-tuple-element.23.arrived_ref, f32[64,1152]{1,0:T(8,128)S(1)} %get-tuple-element.24.forwarded_ref, f32[32,640]{1,0:T(8,128)S(1)} %get-tuple-element.25.refs_0_, ...), custom_call_target="tpu_custom_call" | custom-call | flops 10000000000 | bytes 4000000 | tf_op jit(solution)/shard_map/cond/branch_0_fun/pallas_call | solution.py:351
  (37 shorter events, 0.4 us)
Async XLA Ops:
  0.6 1.3 copy-start
  1.9 0.9 copy-start.3
  2.8 0.7 copy-start.6
  3.5 0.7 copy-start.10
  4.2 0.7 copy-start.11
  4.8 11.0 %copy-start.12 = (f32[4,28,84]{2,0,1:T(4,128)S(1)}, f32[4,28,84]{2,0,1:T(4,128)}, u32[]{:S(2)}) copy-start(f32[4,28,84]{2,0,1:T(4,128)} %param.25) | copy-start | bytes 112900
  4.8 11.0 %copy-start.14 = (s32[256]{0:T(256)S(1)}, s32[256]{0:T(256)}, u32[]{:S(2)}) copy-start(s32[256]{0:T(256)} %param.22) | copy-start | bytes 3076
  4.8 11.1 %copy-start.13 = (f32[4,84,28]{1,0,2:T(4,128)S(1)}, f32[4,84,28]{1,0,2:T(4,128)}, u32[]{:S(2)}) copy-start(f32[4,84,28]{1,0,2:T(4,128)} %param.26) | copy-start | bytes 112900
  4.8 11.4 %copy-start.1 = (f32[13,84,256]{2,1,0:T(8,128)S(1)}, f32[13,84,256]{2,1,0:T(8,128)}, u32[]{:S(2)}) copy-start(f32[13,84,256]{2,1,0:T(8,128)} %pred_ref.5) | copy-start | bytes 3354628
  4.8 11.4 %copy-start.5 = (s32[4,256]{1,0:T(4,128)S(1)}, s32[4,256]{1,0:T(4,128)}, u32[]{:S(2)}) copy-start(s32[4,256]{1,0:T(4,128)} %link_ref.3) | copy-start | bytes 12292
  4.8 11.4 %copy-start.7 = (s32[256]{0:T(256)S(1)}, s32[256]{0:T(256)}, u32[]{:S(2)}) copy-start(s32[256]{0:T(256)} %param.18) | copy-start | bytes 3076
  5.4 13.4 %collective-permute-start.2 = (f32[8,2304]{1,0:T(8,128)S(1)}, f32[8,2304]{1,0:T(8,128)S(1)}, u32[]{:S(2)}, u32[]{:S(2)}) collective-permute-start(f32[8,2304]{1,0:T(8,128)S(1)} %shard_map.154), channel_id=1, source_target_pairs={{0,3},{1,0},{2,1},{3,2},{4,7},{5,4},{6,5},{7,6},{8,11},{9,8},{10,9... | collective-permute-start | bytes 221192 | tf_op jit(solution)/shard_map/ppermute | solution.py:374
  10.9 7.9 %collective-permute-start.1 = (f32[8,2304]{1,0:T(8,128)S(1)}, f32[8,2304]{1,0:T(8,128)S(1)}, u32[]{:S(2)}, u32[]{:S(2)}) collective-permute-start(f32[8,2304]{1,0:T(8,128)S(1)} %shard_map.154), channel_id=1, source_target_pairs={{0,2},{1,3},{2,0},{3,1},{4,6},{5,7},{6,4},{7,5},{8,10},{9,11},{10,... | collective-permute-start | bytes 221192 | tf_op jit(solution)/shard_map/ppermute | solution.py:374
  13.2 6.3 %collective-permute-start = (f32[8,2304]{1,0:T(8,128)S(1)}, f32[8,2304]{1,0:T(8,128)S(1)}, u32[]{:S(2)}, u32[]{:S(2)}) collective-permute-start(f32[8,2304]{1,0:T(8,128)S(1)} %shard_map.154), channel_id=1, source_target_pairs={{0,1},{1,2},{2,3},{3,0},{4,5},{5,6},{6,7},{7,4},{8,9},{9,10},{10,1... | collective-permute-start | bytes 221192 | tf_op jit(solution)/shard_map/ppermute | solution.py:374
  16.2 12.7 %copy-start.2 = (f32[13,84,256]{2,1,0:T(8,128)S(1)}, f32[13,84,256]{2,1,0:T(8,128)}, u32[]{:S(2)}) copy-start(f32[13,84,256]{2,1,0:T(8,128)} %state_ref.1) | copy-start | bytes 3354628
  16.2 12.7 %copy-start.8 = (s32[256]{0:T(256)S(1)}, s32[256]{0:T(256)}, u32[]{:S(2)}) copy-start(s32[256]{0:T(256)} %param.19) | copy-start | bytes 3076
  16.2 12.7 %copy-start.15 = (f32[3,84,84]{2,1,0:T(8,128)S(1)}, f32[3,84,84]{2,1,0:T(8,128)}, u32[]{:S(2)}) copy-start(f32[3,84,84]{2,1,0:T(8,128)} %der_ref.1) | copy-start | bytes 254020
  19.5 14.5 %collective-permute-start.4 = (f32[32,1664]{1,0:T(8,128)S(1)}, f32[32,1664]{1,0:T(8,128)S(1)}, u32[]{:S(2)}, u32[]{:S(2)}) collective-permute-start(f32[32,1664]{1,0:T(8,128)S(1)} %pad_maximum_fusion), channel_id=1, source_target_pairs={{0,508},{4,0},{8,4},{12,8},{16,12},{20,16},{24,20},{28,24},{32,28}... | collective-permute-start | bytes 638984 | tf_op jit(solution)/shard_map/ppermute | solution.py:377
  27.0 9.4 %collective-permute-start.3 = (f32[32,1664]{1,0:T(8,128)S(1)}, f32[32,1664]{1,0:T(8,128)S(1)}, u32[]{:S(2)}, u32[]{:S(2)}) collective-permute-start(f32[32,1664]{1,0:T(8,128)S(1)} %pad_maximum_fusion), channel_id=1, source_target_pairs={{0,4},{4,8},{8,12},{12,16},{16,20},{20,24},{24,28},{28,32},{32,36}... | collective-permute-start | bytes 638984 | tf_op jit(solution)/shard_map/ppermute | solution.py:376
  34.0 2.5 %copy-start.4 = (f32[3,4,256]{2,1,0:T(4,128)S(1)}, f32[3,4,256]{2,1,0:T(4,128)}, u32[]{:S(2)}) copy-start(f32[3,4,256]{2,1,0:T(4,128)} %normals_ref.1) | copy-start | bytes 36868
  34.0 2.5 %copy-start.9 = (s32[256]{0:T(256)S(1)}, s32[256]{0:T(256)}, u32[]{:S(2)}) copy-start(s32[256]{0:T(256)} %param.23) | copy-start | bytes 3076
  141.3 6.5 %collective-permute-start.5 = (f32[64,1152]{1,0:T(8,128)S(1)}, f32[64,1152]{1,0:T(8,128)S(1)}, u32[]{:S(2)}, u32[]{:S(2)}) collective-permute-start(f32[64,1152]{1,0:T(8,128)S(1)} %get-tuple-element.49), channel_id=1, source_target_pairs={{0,4},{4,0},{8,12},{12,8},{16,20},{20,16},{24,28},{28,24},{32,36},... | collective-permute-start | bytes 884744 | tf_op jit(solution)/shard_map/ppermute | solution.py:424

commit v2 on v1

--- a/solution.py
+++ b/solution.py
@@ -67,24 +67,30 @@
         s_ref[f] = dot(matrices, jnp.concatenate([hi, lo, hi], axis=0).astype(bf16))
 
 
-def apply_jacobian(s_ref, a_ref, half, blocks, finish):
+def apply_jacobian(s_ref, a_ref, half, tiles, finish):
     lanes = pl.ds(half * 128, 128)
 
-    def body(i, carry):
-        r = pl.multiple_of(i * 16, 16)
-        acc = [[None] * F for _ in range(2)]
+    def block(r, count):
+        acc = [[None] * F for _ in range(count)]
         for d in range(3):
             for f in range(F):
-                x = [s_ref[f, pl.ds(d * MS + r + 8 * t, 8), lanes] for t in range(2)]
+                x = [s_ref[f, pl.ds(d * MS + r + 8 * t, 8), lanes] for t in range(count)]
                 for g in range(F):
                     w = jnp.broadcast_to(a_ref[pl.ds(d * AR + g * F + f, 1), lanes], (8, 128))
-                    for t in range(2):
+                    for t in range(count):
                         acc[t][g] = w * x[t] if acc[t][g] is None else acc[t][g] + w * x[t]
-        for t in range(2):
+        for t in range(count):
             finish(pl.multiple_of(r + 8 * t, 8), lanes, acc[t])
+
+    def body(i, carry):
+        block(pl.multiple_of(i * 16, 16), 2)
         return carry
 
-    lax.fori_loop(0, blocks, body, 0)
+    lax.fori_loop(0, tiles // 2, body, 0)
+
+    @pl.when(tiles % 2 == 1)
+    def _():
+        block(pl.multiple_of(tiles // 2 * 16, 16), 1)
 
 
 def material_matrix(jac_ref, onehot):
@@ -172,7 +178,7 @@
             base_ref[g, pl.ds(r, 8), lanes] = base_ref[g, pl.ds(r, 8), lanes] - acc[g]
 
     for half in range(2):
-        apply_jacobian(s, a_ref, half, MP // 16, finish)
+        apply_jacobian(s, a_ref, half, MS // 8, finish)
 
 
 def flux_kernel(
@@ -321,7 +327,7 @@
         x[f] = pad_rows(rows, MP)
         ahead[f] = time_step * pad_rows(rows, MP)
     top = [jnp.max(degree[:, 128 * half : 128 * (half + 1)]) for half in range(2)]
-    blocks = [jnp.where(t <= 2, 1, jnp.where(t == 3, 2, jnp.where(t == 4, 3, jnp.where(t == 5, 4, 6)))) for t in top]
+    tiles = [jnp.where(t <= 2, 2, jnp.where(t == 3, 3, jnp.where(t == 4, 5, jnp.where(t == 5, 7, 11)))) for t in top]
 
     def step(j, factor):
         factor = factor * time_step / (j + 1).astype(f32)
@@ -337,7 +343,7 @@
                     x[g, pl.ds(at, 8), lanes] = t
                     ahead[g, pl.ds(at, 8), lanes] = ahead[g, pl.ds(at, 8), lanes] + weight * t
 
-            apply_jacobian(s, a, half, jnp.where(j <= top[half], blocks[half], 0), finish)
+            apply_jacobian(s, a, half, jnp.where(j <= top[half], tiles[half], 0), finish)
         return factor
 
     lax.fori_loop(1, 7, step, jnp.float32(time_step))
@@ -370,7 +376,7 @@
     core = lax.axis_index("dom").astype(jnp.int32) % 2
     me = jnp.stack([lax.axis_index("narrow").astype(jnp.int32), core])
     row = lambda v: v.reshape(1, E)
-    (mine,) = call(pick_kernel, [(8, PICK + JROWS)], [], 0, [predictor, row(degree), publish.reshape(1, 8), jnp.transpose(jacobians, (1, 2, 0, 3)), speeds.reshape(1, 8)], 10**9, 12)
+    (mine,) = call(pick_kernel, [(8, PICK + JROWS)], [], 0, [predictor, row(degree), publish.reshape(1, 8), jnp.transpose(jacobians, (1, 2, 0, 3)), speeds.reshape(1, 8)], 10**9, 60)
     shared = jnp.concatenate([mine] + [lax.ppermute(mine, "narrow", ring(4, s)) for s in (1, 2, 3)], axis=0)
     picks, jac = shared[:, :PICK], shared[:, PICK:]
     low = lax.ppermute(picks, "dom", ring(128, 1))

time: 172 us -> 169 us (0.983)
  local copies, waits for them, and re-layouts: 4.57 us -> 0.41 us
    unnamed x34 -> x26, local copies, waits for them, and re-layouts: 4.36 us -> 0.2 us
where the time goes in v2:
time: 169 us
  blocking collectives  97 us (57%)
  Pallas kernels  40.6 us (24%)
  starting transfers between devices  25 us (15%)
  waiting for transfers between devices  4.49 us (3%)
    all_to_all x1, blocking collectives, shards(): lax.all_to_all(outgoing, 'dom', split_axis=0, concat_axis=0, tiled=True)  97 us
    pallas_call x6, Pallas kernels, call(): pl.pallas_call(kernel, out_shape=[jax.ShapeDtypeStruct(o, f32) for o in o...  40.6 us
    ppermute x3, starting transfers between devices, shards(): lax.ppermute(mine, 'narrow', ring(4, s))  10.3 us
    ppermute x1, starting transfers between devices, shards(): high = lax.ppermute(picks, 'dom', ring(128, -1))  7.5 us
    ppermute x1, starting transfers between devices, shards(): forwarded = lax.ppermute(forwarded, 'dom', [(i, i ^ 1) for i in range(128)])  5.26 us
  transfers between devices with their start and end apart: 6, of which 3 were waited for; matrix products, arithmetic and copies ran while one was open for 0% of the time, Pallas kernels for 4%

profile of v2, /device:TPU:1, one launch (start us, length us, event | category | flops | bytes accessed | tf_op | source)
XLA Modules:
  0.0 168.6 jit_solution(721350887409352381)
XLA Ops:
  0.7 2.7 %shard_map.154 = f32[8,2304]{1,0:T(8,128)} custom-call(f32[13,84,256]{2,1,0:T(8,128)} %pred_ref.5, s32[1,256]{1,0:T(1,128)} %bitcast.12, s32[1,8]{1,0:T(1,128)} %bitcast.26, f32[3,13,8,13]{3,2,1,0:T(8,128)} %bitcast.25, f32[1,8]{1,0:T(1,128)} %bitcast.27), custom_call_target="tpu_custom_call" | custom-call | flops 1000000000 | bytes 4000000 | tf_op jit(solution)/shard_map/pallas_call | solution.py:357
  3.4 5.5 %collective-permute-start.2 = (f32[8,2304]{1,0:T(8,128)}, f32[8,2304]{1,0:T(8,128)S(1)}, u32[]{:S(2)}, u32[]{:S(2)}) collective-permute-start(f32[8,2304]{1,0:T(8,128)} %shard_map.154), channel_id=1, source_target_pairs={{0,3},{1,0},{2,1},{3,2},{4,7},{5,4},{6,5},{7,6},{8,11},{9,8},{10,9... | collective-permute-start | bytes 221192 | tf_op jit(solution)/shard_map/ppermute | solution.py:380
  8.8 2.3 %collective-permute-start.1 = (f32[8,2304]{1,0:T(8,128)}, f32[8,2304]{1,0:T(8,128)S(1)}, u32[]{:S(2)}, u32[]{:S(2)}) collective-permute-start(f32[8,2304]{1,0:T(8,128)} %shard_map.154), channel_id=1, source_target_pairs={{0,2},{1,3},{2,0},{3,1},{4,6},{5,7},{6,4},{7,5},{8,10},{9,11},{10,... | collective-permute-start | bytes 221192 | tf_op jit(solution)/shard_map/ppermute | solution.py:380
  11.1 2.6 %collective-permute-start = (f32[8,2304]{1,0:T(8,128)}, f32[8,2304]{1,0:T(8,128)S(1)}, u32[]{:S(2)}, u32[]{:S(2)}) collective-permute-start(f32[8,2304]{1,0:T(8,128)} %shard_map.154), channel_id=1, source_target_pairs={{0,1},{1,2},{2,3},{3,0},{4,5},{5,6},{6,7},{7,4},{8,9},{9,10},{10,1... | collective-permute-start | bytes 221192 | tf_op jit(solution)/shard_map/ppermute | solution.py:380
  13.7 0.1 copy.26.owner_col_ref
  13.9 0.1 copy.25.lift_ref
  14.0 0.1 pad.3.clone
  14.1 0.0 copy-start.1
  14.2 0.0 copy-start.5
  14.2 2.5 %shard_map.153 = (f32[4,416,256]{2,1,0:T(8,128)S(1)}, f32[4,416,256]{2,1,0:T(8,128)S(1)}) custom-call(f32[13,84,256]{2,1,0:T(8,128)S(1)} %copy-done, s32[1,256]{1,0:T(1,128)S(1)} %bitcast.13, f32[4,28,84]{2,1,0:T(8,128)S(1)} %copy.23.trace_ref, s32[4,256]{1,0:T(4,128)S(1)} %copy-done.3), custom_call_target="tpu_custom_call" | custom-call | flops 4000000000 | bytes 4000000 | tf_op jit(solution)/shard_map/pallas_call | solution.py:357
  16.7 0.1 pad_add_fusion.me_ref
  16.8 0.8 collective-permute-done
  17.6 7.5 %collective-permute-start.4 = (f32[32,1664]{1,0:T(8,128)S(1)}, f32[32,1664]{1,0:T(8,128)S(1)}, u32[]{:S(2)}, u32[]{:S(2)}) collective-permute-start(f32[32,1664]{1,0:T(8,128)S(1)} %pad_maximum_fusion), channel_id=1, source_target_pairs={{0,508},{4,0},{8,4},{12,8},{16,12},{20,16},{24,20},{28,24},{32,28}... | collective-permute-start | bytes 638984 | tf_op jit(solution)/shard_map/ppermute | solution.py:383
  25.1 1.9 %collective-permute-start.3 = (f32[32,1664]{1,0:T(8,128)S(1)}, f32[32,1664]{1,0:T(8,128)S(1)}, u32[]{:S(2)}, u32[]{:S(2)}) collective-permute-start(f32[32,1664]{1,0:T(8,128)S(1)} %pad_maximum_fusion), channel_id=1, source_target_pairs={{0,4},{4,8},{8,12},{12,16},{16,20},{20,24},{24,28},{28,32},{32,36}... | collective-permute-start | bytes 638984 | tf_op jit(solution)/shard_map/ppermute | solution.py:382
  27.1 4.8 %shard_map.155 = (f32[13,96,256]{2,1,0:T(8,128)S(1)}, f32[640,256]{1,0:T(8,128)S(1)}) custom-call(s32[2]{0:T(128)S(1)} %pad_add_fusion.me_ref, f32[13,84,256]{2,1,0:T(8,128)S(1)} %copy-done.1, f32[13,84,256]{2,1,0:T(8,128)S(1)} %copy-done, s32[1,256]{1,0:T(1,128)S(1)} %bitcast.14, s32[1,256]{1,0:T(1,128)S(1)} %bitcast.16, ...), custom_call_target="tpu_custom_call" | custom-call | flops 4000000000 | bytes 4000000 | tf_op jit(solution)/shard_map/pallas_call | solution.py:357
  32.0 2.5 %collective-permute-done.3 = f32[32,1664]{1,0:T(8,128)S(1)} collective-permute-done((f32[32,1664]{1,0:T(8,128)S(1)}, f32[32,1664]{1,0:T(8,128)S(1)}, u32[]{:S(2)}, u32[]{:S(2)}) %collective-permute-start.3) | collective-permute-done | bytes 213024 | tf_op jit(solution)/shard_map/ppermute | solution.py:382
  34.5 0.1 maximum_maximum_fusion.pick_ref
  34.6 6.7 %shard_map.156 = (f32[128,1,3456]{2,1,0:T(1,128)S(1)}, f32[1152,256]{1,0:T(8,128)}) custom-call(s32[2]{0:T(128)S(1)} %pad_add_fusion.me_ref, f32[4,416,256]{2,1,0:T(8,128)S(1)} %get-tuple-element.43.own_ref, f32[4,416,256]{2,1,0:T(8,128)S(1)} %get-tuple-element.44.near_ref, f32[13,96,256]{2,1,0:T(8,128)S(1)} %get-tuple-element.45.base_ref, ...), custom_call_target="tpu_custom_call" | custom-call | flops 4000000000 | bytes 4000000 | tf_op jit(solution)/shard_map/pallas_call | solution.py:357
  41.4 97.0 %all_to_all.10.arrived_ref = f32[128,1,3456]{2,1,0:T(1,128)S(1)} all-to-all(f32[128,1,3456]{2,1,0:T(1,128)S(1)} %get-tuple-element.47), channel_id=1, replica_groups=mesh['dom'=128,'narrow'=4] {'dom'}, dimensions={0} | all-to-all | bytes 3538944 | tf_op jit(solution)/shard_map/all_to_all | solution.py:428
  138.4 0.9 shard_map.157
  139.3 5.3 %collective-permute-start.5 = (f32[64,1152]{1,0:T(8,128)S(1)}, f32[64,1152]{1,0:T(8,128)S(1)}, u32[]{:S(2)}, u32[]{:S(2)}) collective-permute-start(f32[64,1152]{1,0:T(8,128)S(1)} %get-tuple-element.49), channel_id=1, source_target_pairs={{0,4},{4,0},{8,12},{12,8},{16,20},{20,16},{24,28},{28,24},{32,36},... | collective-permute-start | bytes 884744 | tf_op jit(solution)/shard_map/ppermute | solution.py:430
  144.6 1.2 collective-permute-done.5
  145.8 22.9 %conditional.1 = ((f32[13,84,256]{2,1,0:T(8,128)}, f32[13,84,256]{2,1,0:T(8,128)})) conditional(s32[]{:T(128)} %bitcast.10, (s32[2]{0:T(128)S(1)}, f32[128,1,3456]{2,1,0:T(1,128)S(1)}, f32[64,1152]{1,0:T(8,128)S(1)}, f32[32,640]{1,0:T(8,128)S(1)}, f32[3,84,84]{2,1,0:T(8,128)S(1)}) %tuple.26, (f32[1152,256]{1,0:T(8,128)}, s32[1,256]{1,0:T(1,128)S(1)}, ...), branch_computations={%region_0.1_spmd, %region_1.2_spmd} | conditional | flops 11000000512 | bytes 22157832 | solution.py:444
  145.8 22.9 %branch_0_fun.1 = (f32[13,84,256]{2,1,0:T(8,128)}, f32[13,84,256]{2,1,0:T(8,128)}) custom-call(s32[2]{0:T(128)S(1)} %get-tuple-element.22.me_ref, f32[128,1,3456]{2,1,0:T(1,128)S(1)} %get-tuple-element.23.arrived_ref, f32[64,1152]{1,0:T(8,128)S(1)} %get-tuple-element.24.forwarded_ref, f32[32,640]{1,0:T(8,128)S(1)} %get-tuple-element.25.refs_0_, ...), custom_call_target="tpu_custom_call" | custom-call | flops 10000000000 | bytes 4000000 | tf_op jit(solution)/shard_map/cond/branch_0_fun/pallas_call | solution.py:357
  (29 shorter events, 0.1 us)
Async XLA Ops:
  0.6 13.1 %copy-start.8 = (f32[4,28,84]{2,0,1:T(4,128)S(1)}, f32[4,28,84]{2,0,1:T(4,128)}, u32[]{:S(2)}) copy-start(f32[4,28,84]{2,0,1:T(4,128)} %param.25) | copy-start | bytes 112900
  0.6 13.1 %copy-start.10 = (s32[256]{0:T(256)S(1)}, s32[256]{0:T(256)}, u32[]{:S(2)}) copy-start(s32[256]{0:T(256)} %param.22) | copy-start | bytes 3076
  0.7 13.2 %copy-start.9 = (f32[4,84,28]{1,0,2:T(4,128)S(1)}, f32[4,84,28]{1,0,2:T(4,128)}, u32[]{:S(2)}) copy-start(f32[4,84,28]{1,0,2:T(4,128)} %param.26) | copy-start | bytes 112900
  0.7 13.5 %copy-start = (f32[13,84,256]{2,1,0:T(8,128)S(1)}, f32[13,84,256]{2,1,0:T(8,128)}, u32[]{:S(2)}) copy-start(f32[13,84,256]{2,1,0:T(8,128)} %pred_ref.5) | copy-start | bytes 3354628
  0.7 13.5 %copy-start.3 = (s32[4,256]{1,0:T(4,128)S(1)}, s32[4,256]{1,0:T(4,128)}, u32[]{:S(2)}) copy-start(s32[4,256]{1,0:T(4,128)} %link_ref.3) | copy-start | bytes 12292
  0.7 13.4 %copy-start.4 = (s32[256]{0:T(256)S(1)}, s32[256]{0:T(256)}, u32[]{:S(2)}) copy-start(s32[256]{0:T(256)} %param.18) | copy-start | bytes 3076
  3.4 13.4 %collective-permute-start.2 = (f32[8,2304]{1,0:T(8,128)}, f32[8,2304]{1,0:T(8,128)S(1)}, u32[]{:S(2)}, u32[]{:S(2)}) collective-permute-start(f32[8,2304]{1,0:T(8,128)} %shard_map.154), channel_id=1, source_target_pairs={{0,3},{1,0},{2,1},{3,2},{4,7},{5,4},{6,5},{7,6},{8,11},{9,8},{10,9... | collective-permute-start | bytes 221192 | tf_op jit(solution)/shard_map/ppermute | solution.py:380
  8.8 7.9 %collective-permute-start.1 = (f32[8,2304]{1,0:T(8,128)}, f32[8,2304]{1,0:T(8,128)S(1)}, u32[]{:S(2)}, u32[]{:S(2)}) collective-permute-start(f32[8,2304]{1,0:T(8,128)} %shard_map.154), channel_id=1, source_target_pairs={{0,2},{1,3},{2,0},{3,1},{4,6},{5,7},{6,4},{7,5},{8,10},{9,11},{10,... | collective-permute-start | bytes 221192 | tf_op jit(solution)/shard_map/ppermute | solution.py:380
  11.1 6.5 %collective-permute-start = (f32[8,2304]{1,0:T(8,128)}, f32[8,2304]{1,0:T(8,128)S(1)}, u32[]{:S(2)}, u32[]{:S(2)}) collective-permute-start(f32[8,2304]{1,0:T(8,128)} %shard_map.154), channel_id=1, source_target_pairs={{0,1},{1,2},{2,3},{3,0},{4,5},{5,6},{6,7},{7,4},{8,9},{9,10},{10,1... | collective-permute-start | bytes 221192 | tf_op jit(solution)/shard_map/ppermute | solution.py:380
  14.1 3.5 %copy-start.7 = (f32[8,2304]{1,0:T(8,128)S(1)}, f32[8,2304]{1,0:T(8,128)}, u32[]{:S(2)}) copy-start(f32[8,2304]{1,0:T(8,128)} %shard_map.154) | copy-start | bytes 221188
  14.1 12.9 %copy-start.1 = (f32[13,84,256]{2,1,0:T(8,128)S(1)}, f32[13,84,256]{2,1,0:T(8,128)}, u32[]{:S(2)}) copy-start(f32[13,84,256]{2,1,0:T(8,128)} %state_ref.1) | copy-start | bytes 3354628
  14.2 12.9 %copy-start.5 = (s32[256]{0:T(256)S(1)}, s32[256]{0:T(256)}, u32[]{:S(2)}) copy-start(s32[256]{0:T(256)} %param.19) | copy-start | bytes 3076
  14.2 12.9 %copy-start.11 = (f32[3,84,84]{2,1,0:T(8,128)S(1)}, f32[3,84,84]{2,1,0:T(8,128)}, u32[]{:S(2)}) copy-start(f32[3,84,84]{2,1,0:T(8,128)} %der_ref.1) | copy-start | bytes 254020
  17.6 14.4 %collective-permute-start.4 = (f32[32,1664]{1,0:T(8,128)S(1)}, f32[32,1664]{1,0:T(8,128)S(1)}, u32[]{:S(2)}, u32[]{:S(2)}) collective-permute-start(f32[32,1664]{1,0:T(8,128)S(1)} %pad_maximum_fusion), channel_id=1, source_target_pairs={{0,508},{4,0},{8,4},{12,8},{16,12},{20,16},{24,20},{28,24},{32,28}... | collective-permute-start | bytes 638984 | tf_op jit(solution)/shard_map/ppermute | solution.py:383
  25.1 9.4 %collective-permute-start.3 = (f32[32,1664]{1,0:T(8,128)S(1)}, f32[32,1664]{1,0:T(8,128)S(1)}, u32[]{:S(2)}, u32[]{:S(2)}) collective-permute-start(f32[32,1664]{1,0:T(8,128)S(1)} %pad_maximum_fusion), channel_id=1, source_target_pairs={{0,4},{4,8},{8,12},{12,16},{16,20},{20,24},{24,28},{28,32},{32,36}... | collective-permute-start | bytes 638984 | tf_op jit(solution)/shard_map/ppermute | solution.py:382
  32.0 2.7 %copy-start.2 = (f32[3,4,256]{2,1,0:T(4,128)S(1)}, f32[3,4,256]{2,1,0:T(4,128)}, u32[]{:S(2)}) copy-start(f32[3,4,256]{2,1,0:T(4,128)} %normals_ref.1) | copy-start | bytes 36868
  32.0 2.7 %copy-start.6 = (s32[256]{0:T(256)S(1)}, s32[256]{0:T(256)}, u32[]{:S(2)}) copy-start(s32[256]{0:T(256)} %param.23) | copy-start | bytes 3076
  139.3 6.5 %collective-permute-start.5 = (f32[64,1152]{1,0:T(8,128)S(1)}, f32[64,1152]{1,0:T(8,128)S(1)}, u32[]{:S(2)}, u32[]{:S(2)}) collective-permute-start(f32[64,1152]{1,0:T(8,128)S(1)} %get-tuple-element.49), channel_id=1, source_target_pairs={{0,4},{4,0},{8,12},{12,8},{16,20},{20,16},{24,28},{28,24},{32,36},... | collective-permute-start | bytes 884744 | tf_op jit(solution)/shard_map/ppermute | solution.py:430
